TPU v7x, 512 devices: a whole 4x8x8 slice. The times are simulated.
512 devices in a mesh: dp: 16 (over z_hi, x, core), ctx: 32 (over y, z_lo).
Axes of the slice: x: 4, y: 8, z: 8 (z_hi: 2, z_lo: 4; z = z_hi * 4 + z_lo), core: 2. Of those that a mesh axis runs over, the one named last changes fastest.
Arguments:
- queries: bfloat16 [16, 16384, 512], P('dp', 'ctx'), may hold values from -36 to 36
- keys: bfloat16 [16, 16384, 512], P('dp', 'ctx'), may hold values from -36 to 36
- values: bfloat16 [16, 16384, 512], P('dp', 'ctx'), may hold values from -6 to 6
- grad_out: bfloat16 [16, 16384, 512], P('dp', 'ctx'), may hold values from -48 to 48
- gains: float32 [2, 512], replicated, may hold values from 0.1 to 1.9
Outputs:
- grad_queries: bfloat16 [16, 16384, 512], P('dp', 'ctx')
- grad_keys: bfloat16 [16, 16384, 512], P('dp', 'ctx')
- grad_values: bfloat16 [16, 16384, 512], P('dp', 'ctx')
- gain_grads: float32 [2, 512], P(None, 'dp')
All inputs are finite; a program needn't handle non-finite values.
Results may differ from a plain program's by a relative error of at most 0.0093.
Values may be sent and summed in bfloat16 or wider, within the bound.
A program may use at most 64 MiB of HBM per device.

v0:
```python
import math
import jax
import jax.numpy as jnp
from jax import lax
from jax.sharding import PartitionSpec as P

HEADS = 4
HD = 128
SPAN = 1
norm_eps = 1e-06


def from_behind(shard, axis, by):
    length = lax.axis_size(axis)
    pairs = [(i, i + by) for i in range(length) if 0 <= i + by < length]
    return lax.ppermute(shard, axis, pairs)


def unit_rows(inputs, heads):
    count = inputs.shape[0]
    wide = inputs.astype(jnp.float32).reshape(count, heads, -1)
    inverse = lax.rsqrt(jnp.mean(wide * wide, axis=2, keepdims=True) + norm_eps)
    return (wide * inverse, inverse)


def norm_backward(grad_norm, unit, inverse, gain):
    count, heads, head_dim = unit.shape
    grad_three = grad_norm.reshape(count, heads, head_dim)
    scaled = grad_three * gain
    mean_term = jnp.mean(scaled * unit, axis=2, keepdims=True)
    grad_in = inverse * (scaled - unit * mean_term)
    gain_grad = jnp.sum(grad_three * unit, axis=0).reshape(-1)
    return (grad_in.reshape(count, -1).astype(jnp.bfloat16), gain_grad)


def cross(left, right):
    return jnp.einsum("ad,cd->ac", left, right, preferred_element_type=jnp.float32)


def inner(left, right):
    return jnp.einsum("ac,ad->cd", left, right, preferred_element_type=jnp.float32)


def per_device(queries, keys, values, grad_out, gains):
    heads = HEADS
    head_dim = HD
    span = SPAN
    rows = queries.shape[1]
    reach = span * rows
    scale = 1.0 / math.sqrt(head_dim)
    place = lax.axis_index("ctx")
    q_unit, q_inv = unit_rows(queries[0], heads)
    k_unit, k_inv = unit_rows(keys[0], heads)
    q_gain = gains[0].reshape(heads, head_dim)
    k_gain = gains[1].reshape(heads, head_dim)
    q_norm = (q_unit * q_gain).reshape(rows, -1).astype(jnp.bfloat16)
    k_norm = (k_unit * k_gain).reshape(rows, -1).astype(jnp.bfloat16)
    upstream = grad_out[0]
    own = jnp.stack([k_norm, values[0]])
    tiles = [own]
    step = 1
    tiles.append(from_behind(own, "ctx", step))
    window = jnp.concatenate(tiles[::-1], axis=1)
    query_pos = lax.broadcasted_iota(jnp.int32, (rows, (span + 1) * rows), 0)
    key_pos = lax.broadcasted_iota(jnp.int32, (rows, (span + 1) * rows), 1)
    visible = (
        (key_pos > query_pos) & (key_pos <= query_pos + reach) & (key_pos >= (span - place) * rows)
    )
    first_key = 0
    dq_parts, dk_parts, dv_parts, lse_parts, delta_parts = ([], [], [], [], [])
    for head in range(heads):
        cols = slice(head * head_dim, (head + 1) * head_dim)
        q_head = q_norm[:, cols]
        k_head = window[0, :, cols]
        v_head = window[1, :, cols]
        g_head = upstream[:, cols]
        scores = cross(q_head, k_head) * scale
        total = jnp.sum(jnp.where(visible, jnp.exp(scores), 0.0), axis=1, keepdims=True)
        log_total = jnp.log(total)
        probs = jnp.where(visible, jnp.exp(scores - log_total), 0.0)
        probs_low = probs.astype(jnp.bfloat16)
        attended = jnp.dot(probs_low, v_head, preferred_element_type=jnp.float32)
        delta = jnp.sum(g_head.astype(jnp.float32) * attended, axis=1, keepdims=True)
        grad_scores = (probs * (cross(g_head, v_head) - delta)).astype(jnp.bfloat16)
        dq_parts.append(jnp.dot(grad_scores, k_head, preferred_element_type=jnp.float32) * scale)
        dk_parts.append(inner(grad_scores, q_head) * scale)
        dv_parts.append(inner(probs_low, g_head))
        lse_parts.append(log_total[:, 0])
        delta_parts.append(delta[:, 0])
    grad_qn = jnp.concatenate(dq_parts, axis=1)
    key_grads = jnp.stack([jnp.concatenate(dk_parts, axis=1), jnp.concatenate(dv_parts, axis=1)])
    local = key_grads[:, span * rows :]
    step = 1
    term = key_grads[:, (span - step) * rows : (span - step + 1) * rows]
    local = local + from_behind(term, "ctx", -step)
    grad_queries, q_gain_grad = norm_backward(grad_qn, q_unit, q_inv, q_gain)
    grad_keys, k_gain_grad = norm_backward(local[0], k_unit, k_inv, k_gain)
    grad_values = local[1].astype(jnp.bfloat16)
    gain_terms = jnp.stack([q_gain_grad, k_gain_grad])
    gain_total = lax.psum(gain_terms, "ctx")
    gain_share = lax.psum_scatter(gain_total, "dp", scatter_dimension=1, tiled=True)
    return (grad_queries[None], grad_keys[None], grad_values[None], gain_share)


def solution(mesh):
    placed = (
        P("dp", "ctx", None),
        P("dp", "ctx", None),
        P("dp", "ctx", None),
        P("dp", "ctx", None),
        P(),
    )
    return jax.shard_map(
        per_device,
        mesh=mesh,
        in_specs=placed,
        out_specs=(P("dp", "ctx", None), P("dp", "ctx", None), P("dp", "ctx", None), P(None, "dp")),
        check_vma=False,
    )
```

profile of v0, /device:TPU:2, one launch (start us, length us, event | category | flops | bytes accessed | tf_op | source)
XLA Modules:
  0.0 287.6 jit_solution(17089914442977109020)
XLA Ops:
  7.2 0.8 fusion.47
  8.0 1.3 copy.21
  9.2 1.3 copy.22
  10.5 1.2 multiply_reduce_fusion.3
  11.8 1.1 pad_maximum_fusion.1
  13.0 5.3 %collective-permute-start = (bf16[2,512,512]{1,2,0:T(8,128)(2,1)}, bf16[2,512,512]{1,2,0:T(8,128)(2,1)}, u32[]{:S(2)}, u32[]{:S(2)}) collective-permute-start(bf16[2,512,512]{1,2,0:T(8,128)(2,1)} %pad_maximum_fusion.1), channel_id=1, source_target_pairs={{0,1},{1,2},{2,3},{3,4},{4,5},{5,6},{6,7},{7,8},{8,9},{9,10},{10,1... | collective-permute-start | bytes 3145736 | tf_op jit(solution)/shard_map/ppermute | solution.py:16
  18.4 1.3 copy.23
  20.1 19.8 %collective-permute-done = bf16[2,512,512]{1,2,0:T(8,128)(2,1)} collective-permute-done((bf16[2,512,512]{1,2,0:T(8,128)(2,1)}, bf16[2,512,512]{1,2,0:T(8,128)(2,1)}, u32[]{:S(2)}, u32[]{:S(2)}) %collective-permute-start) | collective-permute-done | bytes 1048608 | tf_op jit(solution)/shard_map/ppermute | solution.py:16
  40.0 1.5 maximum_maximum_fusion
  41.5 0.5 fusion.26
  42.0 0.5 fusion.25
  42.4 0.5 fusion.24
  42.9 2.0 select_reduce_fusion.3
  44.9 2.4 fusion.8
  47.4 0.5 fusion.12
  47.9 0.3 fusion.44
  48.2 0.5 fusion.14
  48.7 0.3 fusion.38
  49.0 0.5 fusion.13
  49.5 0.3 fusion.41
  49.8 0.5 fusion.15
  50.3 0.3 fusion.35
  50.6 1.0 fusion.5
  51.6 1.0 fusion.3
  52.7 1.0 fusion.4
  53.7 1.0 fusion.2
  54.7 0.3 convolution_multiply_fusion
  55.0 0.3 convolution_multiply_fusion.2
  55.3 0.3 convolution_multiply_fusion.3
  55.6 0.3 convolution_multiply_fusion.1
  55.9 0.6 maximum_bitcast_fusion
  56.8 1.5 collective-permute-start.1
  58.3 0.5 convolution_multiply_fusion.4
  58.8 0.5 convolution_multiply_fusion.8
  59.3 0.5 convolution_multiply_fusion.6
  59.8 0.5 convolution_multiply_fusion.10
  60.6 0.4 fusion.19
  61.0 44.9 %collective-permute-done.1 = f32[2,512,512]{1,2,0:T(8,128)S(1)} collective-permute-done((f32[2,512,512]{1,2,0:T(8,128)S(1)}, f32[2,512,512]{1,2,0:T(8,128)S(1)}, u32[]{:S(2)}, u32[]{:S(2)}) %collective-permute-start.1) | collective-permute-done | bytes 2097184 | tf_op jit(solution)/shard_map/ppermute | solution.py:16
  105.9 0.5 fusion.1
  106.5 1.1 copy-done
  107.9 1.1 multiply_reduce_fusion
  109.0 0.9 copy.35
  109.9 1.0 copy.28
  111.0 1.0 copy.30
  112.0 1.0 copy.29
  113.0 88.8 %reduce-scatter.4.cloned.1.call-done = f32[32,2]{1,0:T(8,128)} async-done(((f32[512,2]{1,0:T(8,128)}), f32[32,2]{1,0:T(8,128)}) %reduce-scatter.4.cloned.1.call-update) | async-done | bytes 272
  201.8 0.8 copy.36
  202.5 78.3 %psum.8 = f32[2,32]{1,0:T(2,128)} all-reduce(f32[2,32]{1,0:T(2,128)S(1)} %copy.36), channel_id=1, replica_groups=mesh['dp'=16,'ctx'=32] {'ctx'}, use_global_device_ids=true, to_apply=%region_14.15 | all-reduce | flops 64 | bytes 512 | tf_op jit(solution)/shard_map/psum | solution.py:100
  (28 shorter events, 1.8 us)
Async XLA Ops:
  7.2 194.6 %reduce-scatter.4.cloned.1.call-start = ((), (), s32[]{:S(2)}) async-start(), calls=%async_computation.1 | async-start | bytes 278528
  10.5 7.7 %copy-start.2 = (bf16[1,512,512]{2,1,0:T(8,128)(2,1)S(1)}, bf16[1,512,512]{2,1,0:T(8,128)(2,1)}, u32[]{:S(2)}) copy-start(bf16[1,512,512]{2,1,0:T(8,128)(2,1)} %param.5) | copy-start | bytes 1572868
  13.0 27.0 %collective-permute-start = (bf16[2,512,512]{1,2,0:T(8,128)(2,1)}, bf16[2,512,512]{1,2,0:T(8,128)(2,1)}, u32[]{:S(2)}, u32[]{:S(2)}) collective-permute-start(bf16[2,512,512]{1,2,0:T(8,128)(2,1)} %pad_maximum_fusion.1), channel_id=1, source_target_pairs={{0,1},{1,2},{2,3},{3,4},{4,5},{5,6},{6,7},{7,8},{8,9},{9,10},{10,1... | collective-permute-start | bytes 3145736 | tf_op jit(solution)/shard_map/ppermute | solution.py:16
  56.8 49.1 %collective-permute-start.1 = (f32[2,512,512]{1,2,0:T(8,128)S(1)}, f32[2,512,512]{1,2,0:T(8,128)S(1)}, u32[]{:S(2)}, u32[]{:S(2)}) collective-permute-start(f32[2,512,512]{1,2,0:T(8,128)S(1)} %pad_maximum_fusion), channel_id=1, source_target_pairs={{1,0},{2,1},{3,2},{4,3},{5,4},{6,5},{7,6},{8,7},{9,8},{10,9},{11,1... | collective-permute-start | bytes 6291464 | tf_op jit(solution)/shard_map/ppermute | solution.py:16
  106.4 1.2 copy-start
  110.9 1.1 copy-start.1
Sparse Core Ops, SparseCore 0:
  110.0 91.6 reduce-scatter.3
where the time goes:
time: 288 us
  waiting for transfers between devices  154 us (53%)
  blocking collectives  78.3 us (27%)
  between operations  14.4 us (5%)
  matrix products  13.8 us (5%)
  local copies, waits for them, and re-layouts  10.7 us (4%)
  other arithmetic  10.2 us (4%)
  starting transfers between devices  6.81 us (2%)
    unnamed x2, waiting for transfers between devices  88.8 us
    psum x1, blocking collectives, per_device(): gain_total = lax.psum(gain_terms, 'ctx')  78.3 us
    ppermute x2, waiting for transfers between devices, from_behind(): return lax.ppermute(shard, axis, pairs)  64.8 us
    unnamed x15, local copies, waits for them, and re-layouts  9.78 us
    dot_general x8, matrix products, cross(): jnp.einsum('ad,cd->ac', left, right, preferred_element_type=jnp.float32)  7.34 us
    ppermute x2, starting transfers between devices, from_behind(): return lax.ppermute(shard, axis, pairs)  6.77 us
  transfers between devices with their start and end apart: 3, of which 3 were waited for; matrix products, arithmetic and copies ran while one was open for 3% of the time, Pallas kernels for 0%

commit v1 on v0

--- a/solution.py
+++ b/solution.py
@@ -97,7 +97,7 @@
     grad_keys, k_gain_grad = norm_backward(local[0], k_unit, k_inv, k_gain)
     grad_values = local[1].astype(jnp.bfloat16)
     gain_terms = jnp.stack([q_gain_grad, k_gain_grad])
-    gain_total = lax.psum(gain_terms, "ctx")
+    gain_total = lax.all_gather(gain_terms, axis_name="ctx").sum(axis=0)
     gain_share = lax.psum_scatter(gain_total, "dp", scatter_dimension=1, tiled=True)
     return (grad_queries[None], grad_keys[None], grad_values[None], gain_share)
 

time: 288 us -> 288 us (level)
  the two profiles are of different devices: /device:TPU:2 before, /device:TPU:8 now
where the time goes in v1:
time: 288 us
  waiting for transfers between devices  162 us (56%)
  blocking collectives  68.1 us (24%)
  between operations  14.4 us (5%)
  matrix products  13.8 us (5%)
  local copies, waits for them, and re-layouts  11.3 us (4%)
  other arithmetic  10.3 us (4%)
  starting transfers between devices  8.17 us (3%)
    unnamed x2, waiting for transfers between devices  94.7 us
    all_gather x1, blocking collectives, per_device(): gain_total = lax.all_gather(gain_terms, axis_name='ctx').sum(axis=0)  68.1 us
    ppermute x2, waiting for transfers between devices, from_behind(): return lax.ppermute(shard, axis, pairs)  67.2 us
    unnamed x15, local copies, waits for them, and re-layouts  10.3 us
    ppermute x2, starting transfers between devices, from_behind(): return lax.ppermute(shard, axis, pairs)  8.14 us
    dot_general x8, matrix products, cross(): jnp.einsum('ad,cd->ac', left, right, preferred_element_type=jnp.float32)  7.34 us
  transfers between devices with their start and end apart: 3, of which 3 were waited for; matrix products, arithmetic and copies ran while one was open for 3% of the time, Pallas kernels for 0%

profile of v1, /device:TPU:8, one launch (start us, length us, event | category | flops | bytes accessed | tf_op | source)
XLA Modules:
  0.0 287.8 jit_solution(108849875713759106)
XLA Ops:
  7.2 0.8 fusion.47
  8.0 1.3 copy.21
  9.2 1.3 copy.22
  10.5 1.2 multiply_reduce_fusion.3
  11.8 1.1 pad_maximum_fusion.1
  13.0 4.3 %collective-permute-start = (bf16[2,512,512]{1,2,0:T(8,128)(2,1)}, bf16[2,512,512]{1,2,0:T(8,128)(2,1)}, u32[]{:S(2)}, u32[]{:S(2)}) collective-permute-start(bf16[2,512,512]{1,2,0:T(8,128)(2,1)} %pad_maximum_fusion.1), channel_id=1, source_target_pairs={{0,1},{1,2},{2,3},{3,4},{4,5},{5,6},{6,7},{7,8},{8,9},{9,10},{10,1... | collective-permute-start | bytes 3145736 | tf_op jit(solution)/shard_map/ppermute | solution.py:16
  17.5 1.3 copy.23
  19.1 25.1 %collective-permute-done = bf16[2,512,512]{1,2,0:T(8,128)(2,1)} collective-permute-done((bf16[2,512,512]{1,2,0:T(8,128)(2,1)}, bf16[2,512,512]{1,2,0:T(8,128)(2,1)}, u32[]{:S(2)}, u32[]{:S(2)}) %collective-permute-start) | collective-permute-done | bytes 1048608 | tf_op jit(solution)/shard_map/ppermute | solution.py:16
  44.2 1.5 maximum_maximum_fusion
  45.7 0.5 fusion.26
  46.2 0.5 fusion.25
  46.7 0.5 fusion.24
  47.1 2.0 select_reduce_fusion.3
  49.2 2.4 fusion.8
  51.6 0.5 fusion.12
  52.1 0.3 fusion.44
  52.4 0.5 fusion.14
  52.9 0.3 fusion.38
  53.2 0.5 fusion.13
  53.8 0.3 fusion.41
  54.1 0.5 fusion.15
  54.6 0.3 fusion.35
  54.9 1.0 fusion.5
  55.9 1.0 fusion.3
  56.9 1.0 fusion.4
  57.9 1.0 fusion.2
  58.9 0.3 convolution_multiply_fusion
  59.2 0.3 convolution_multiply_fusion.2
  59.5 0.3 convolution_multiply_fusion.3
  59.9 0.3 convolution_multiply_fusion.1
  60.2 0.6 maximum_bitcast_fusion
  61.0 3.9 %collective-permute-start.1 = (f32[2,512,512]{1,2,0:T(8,128)S(1)}, f32[2,512,512]{1,2,0:T(8,128)S(1)}, u32[]{:S(2)}, u32[]{:S(2)}) collective-permute-start(f32[2,512,512]{1,2,0:T(8,128)S(1)} %pad_maximum_fusion), channel_id=1, source_target_pairs={{1,0},{2,1},{3,2},{4,3},{5,4},{6,5},{7,6},{8,7},{9,8},{10,9},{11,1... | collective-permute-start | bytes 6291464 | tf_op jit(solution)/shard_map/ppermute | solution.py:16
  64.9 0.5 convolution_multiply_fusion.4
  65.4 0.5 convolution_multiply_fusion.8
  65.9 0.5 convolution_multiply_fusion.6
  66.4 0.5 convolution_multiply_fusion.10
  67.2 0.4 fusion.19
  67.6 42.1 %collective-permute-done.1 = f32[2,512,512]{1,2,0:T(8,128)S(1)} collective-permute-done((f32[2,512,512]{1,2,0:T(8,128)S(1)}, f32[2,512,512]{1,2,0:T(8,128)S(1)}, u32[]{:S(2)}, u32[]{:S(2)}) %collective-permute-start.1) | collective-permute-done | bytes 2097184 | tf_op jit(solution)/shard_map/ppermute | solution.py:16
  109.7 0.5 fusion.1
  110.3 1.1 copy-done
  111.7 1.1 multiply_reduce_fusion
  112.9 68.1 %all-gather.1 = f32[32,2,512]{2,1,0:T(2,128)S(1)} all-gather(f32[1,2,512]{2,1,0:T(2,128)S(1)} %maximum_bitcast_fusion.2), channel_id=2, replica_groups=mesh['dp'=16,'ctx'=32] {'ctx'}, dimensions={0}, use_global_device_ids=true | all-gather | bytes 135168 | tf_op jit(solution)/shard_map/all_gather | solution.py:100
  181.0 0.9 copy.35
  181.9 1.0 copy.28
  182.9 1.0 copy.30
  183.9 1.0 copy.29
  184.9 94.7 %reduce-scatter.4.cloned.1.call-done = f32[32,2]{1,0:T(8,128)} async-done(((f32[512,2]{1,0:T(8,128)}), f32[32,2]{1,0:T(8,128)}) %reduce-scatter.4.cloned.1.call-update) | async-done | bytes 272
  279.6 1.4 copy.36
  (29 shorter events, 1.9 us)
Async XLA Ops:
  7.2 272.5 %reduce-scatter.4.cloned.1.call-start = ((), (), s32[]{:S(2)}) async-start(), calls=%async_computation.1 | async-start | bytes 278528
  10.5 6.8 %copy-start.2 = (bf16[1,512,512]{2,1,0:T(8,128)(2,1)S(1)}, bf16[1,512,512]{2,1,0:T(8,128)(2,1)}, u32[]{:S(2)}) copy-start(bf16[1,512,512]{2,1,0:T(8,128)(2,1)} %param.5) | copy-start | bytes 1572868
  13.0 31.2 %collective-permute-start = (bf16[2,512,512]{1,2,0:T(8,128)(2,1)}, bf16[2,512,512]{1,2,0:T(8,128)(2,1)}, u32[]{:S(2)}, u32[]{:S(2)}) collective-permute-start(bf16[2,512,512]{1,2,0:T(8,128)(2,1)} %pad_maximum_fusion.1), channel_id=1, source_target_pairs={{0,1},{1,2},{2,3},{3,4},{4,5},{5,6},{6,7},{7,8},{8,9},{9,10},{10,1... | collective-permute-start | bytes 3145736 | tf_op jit(solution)/shard_map/ppermute | solution.py:16
  61.0 48.7 %collective-permute-start.1 = (f32[2,512,512]{1,2,0:T(8,128)S(1)}, f32[2,512,512]{1,2,0:T(8,128)S(1)}, u32[]{:S(2)}, u32[]{:S(2)}) collective-permute-start(f32[2,512,512]{1,2,0:T(8,128)S(1)} %pad_maximum_fusion), channel_id=1, source_target_pairs={{1,0},{2,1},{3,2},{4,3},{5,4},{6,5},{7,6},{8,7},{9,8},{10,9},{11,1... | collective-permute-start | bytes 6291464 | tf_op jit(solution)/shard_map/ppermute | solution.py:16
  110.2 1.2 copy-start
  182.9 1.1 copy-start.1
Sparse Core Ops, SparseCore 0:
  182.0 97.6 reduce-scatter.3
